TPU v7x, 32 devices: a whole 2x2x4 slice. The times are simulated.
32 devices in a mesh: grp: 2 (over y), seq: 4 (over z), head: 2 (over x), rep: 2 (over core).
Axes of the slice: x: 2, y: 2, z: 4, core: 2. Of those that a mesh axis runs over, the one named last changes fastest.
Arguments:
- activations: bfloat16 [16384, 4096], P(('grp', 'seq', 'rep'), 'head'), parts along dimension 0, may hold values from -6 to 6
- cotangent: bfloat16 [16384, 4096], P(('grp', 'seq', 'rep'), 'head'), parts along dimension 0, may hold values from -6 to 6
- b_proj: bfloat16 [16384, 128], P(('grp', 'seq', 'rep')), parts along dimension 0, may hold values from -6 to 6
- c_proj: bfloat16 [16384, 128], P(('grp', 'seq', 'rep')), parts along dimension 0, may hold values from -0.5 to 0.5
- dt_raw: float32 [32, 16384], P('head', ('grp', 'seq', 'rep')), parts along dimension 1, may hold values from -5.2 to -3.8
- resets: int32 [16384], P(('grp', 'seq', 'rep')), parts along dimension 0, may hold values 0 or 1
- agents: int32 [16384], P(('grp', 'seq', 'rep')), parts along dimension 0, may hold values from 0 to 63
- agent_bias: float32 [32, 64], P('head'), may hold values from -0.7 to 0.7
- a_log: float32 [32], P('head'), may hold values from -9.5 to 1.5
- d_skip: float32 [32], P('head'), may hold values from 0.5 to 2
Outputs:
- grad_input: bfloat16 [16384, 4096], P(('grp', 'seq', 'rep'), 'head'), parts along dimension 0
- grad_b: float32 [16384, 128], P(('grp', 'seq', 'rep')), parts along dimension 0
- grad_c: float32 [16384, 128], P(('grp', 'seq', 'rep')), parts along dimension 0
- grad_rate: float32 [32, 16384], P('head', ('grp', 'seq', 'rep')), parts along dimension 1
There are 2 independent parts, one for each index of `grp`. A program takes and returns all parts, laid end to end along the dimension named above; an argument that names none is the same for every part. Nothing has to cross between parts.
All inputs are finite; a program needn't handle non-finite values. No bound on the sum of `resets` on one device may be relied on, other than what follows from the above.
Results may differ from a plain program's by a relative error of at most 0.01.
Values sent between devices are 32-bit elements; how exact they have to be, the bound alone decides.
A program may use at most 256 MiB of HBM per device.

v0:
```python
from functools import partial

import jax
import jax.numpy as jnp
from jax import lax
from jax.sharding import PartitionSpec as P

BLOCK = 256


def entering(value, axis, join, neutral, backward):
    count, mine = (lax.axis_size(axis), lax.axis_index(axis))
    pieces = jax.tree.map(lambda part: lax.all_gather(part, axis), value)
    if backward:
        pieces = jax.tree.map(lambda part: part[::-1], pieces)
        mine = count - 1 - mine
    subtotal = jax.tree.map(
        lambda part, zero: jnp.full_like(part, 0) + jnp.asarray(zero, part.dtype), value, neutral
    )

    def lap(position, subtotal):
        longer = join(subtotal, jax.tree.map(lambda part: part[position], pieces))
        return jax.tree.map(lambda new, old: jnp.where(position < mine, new, old), longer, subtotal)

    return lax.fori_loop(0, count - 1, lap, subtotal)


def block_terms(carried, pieces, rate, d_skip):
    x_blk, b_blk, c_blk, raw_blk, bias_blk, reset_blk = pieces
    head_count = carried.shape[0]
    head_width = carried.shape[1]
    length = x_blk.shape[0]
    x_heads = x_blk.reshape(length, head_count, head_width)
    step_size = jax.nn.softplus(raw_blk + bias_blk)
    log_decay = -rate[:, None] * step_size
    cumulative = jnp.cumsum(log_decay, axis=1)
    episode = jnp.cumsum(reset_blk)
    position = jnp.arange(length)
    causal = (position[:, None] >= position[None, :]) & (episode[:, None] == episode[None, :])
    log_gap = cumulative[:, :, None] - cumulative[:, None, :]
    within = jnp.where(causal[None], jnp.exp(jnp.where(causal[None], log_gap, 0.0)), 0.0)
    scores = jnp.dot(
        c_blk, b_blk.T, precision=lax.Precision.HIGHEST, preferred_element_type=jnp.float32
    )
    mixing = (scores[None] * within * step_size[:, None, :]).astype(jnp.bfloat16)
    intra_part = jnp.einsum("hij,jhp->ihp", mixing, x_heads, preferred_element_type=jnp.float32)
    entry_decay = jnp.exp(cumulative) * (episode == 0).astype(jnp.float32)[None, :]
    c_scaled = (entry_decay[:, :, None] * c_blk[None]).astype(jnp.bfloat16)
    inter_part = jnp.einsum(
        "hin,hpn->ihp", c_scaled, carried.astype(jnp.bfloat16), preferred_element_type=jnp.float32
    )
    skip_part = d_skip[None, :, None] * x_heads.astype(jnp.float32)
    output = (
        (intra_part + inter_part + skip_part)
        .reshape(length, head_count * head_width)
        .astype(jnp.bfloat16)
    )
    same_end = (episode == episode[-1]).astype(jnp.float32)[None, :]
    to_end = jnp.exp(cumulative[:, -1:] - cumulative) * same_end * step_size
    b_scaled = (to_end[:, :, None] * b_blk[None]).astype(jnp.bfloat16)
    added_state = jnp.einsum("jhp,hjn->hpn", x_heads, b_scaled, preferred_element_type=jnp.float32)
    carry_decay = jnp.exp(cumulative[:, -1]) * (episode[-1] == 0).astype(jnp.float32)
    next_state = carry_decay[:, None, None] * carried + added_state
    return (next_state, output)


def block_pieces(activations, b_full, c_full, raw_rates, bias_rates, resets):
    token_count = activations.shape[0]
    head_count = raw_rates.shape[0]
    block_count = token_count // BLOCK
    return (
        activations.reshape(block_count, BLOCK, -1),
        b_full.reshape(block_count, BLOCK, -1),
        c_full.reshape(block_count, BLOCK, -1),
        raw_rates.reshape(head_count, block_count, BLOCK).transpose(1, 0, 2),
        bias_rates.reshape(head_count, block_count, BLOCK).transpose(1, 0, 2),
        resets.reshape(block_count, BLOCK),
    )


def run_blocks(activations, b_full, c_full, raw_rates, bias_rates, resets, rate, d_skip, carried):
    token_count = activations.shape[0]
    pieces = block_pieces(activations, b_full, c_full, raw_rates, bias_rates, resets)
    final_state, block_outputs = lax.scan(
        partial(block_terms, rate=rate, d_skip=d_skip), carried, pieces
    )
    return (block_outputs.reshape(token_count, -1), final_state)


def block_summary(pieces, rate):
    x_blk, b_blk, c_blk, raw_blk, bias_blk, reset_blk, cot_blk = pieces
    head_count = raw_blk.shape[0]
    length = x_blk.shape[0]
    x_heads = x_blk.reshape(length, head_count, -1)
    cot_heads = cot_blk.reshape(length, head_count, -1)
    step_size = jax.nn.softplus(raw_blk + bias_blk)
    cumulative = jnp.cumsum(-rate[:, None] * step_size, axis=1)
    episode = jnp.cumsum(reset_blk)
    same_end = (episode == episode[-1]).astype(jnp.float32)[None, :]
    to_end = jnp.exp(cumulative[:, -1:] - cumulative) * same_end * step_size
    b_scaled = (to_end[:, :, None] * b_blk[None]).astype(jnp.bfloat16)
    added_state = jnp.einsum("jhp,hjn->hpn", x_heads, b_scaled, preferred_element_type=jnp.float32)
    carry_decay = jnp.exp(cumulative[:, -1]) * (episode[-1] == 0).astype(jnp.float32)
    entry_decay = jnp.exp(cumulative) * (episode == 0).astype(jnp.float32)[None, :]
    c_scaled = (entry_decay[:, :, None] * c_blk[None]).astype(jnp.bfloat16)
    inject = jnp.einsum("ihp,hin->hpn", cot_heads, c_scaled, preferred_element_type=jnp.float32)
    inject = inject.astype(jnp.bfloat16).astype(jnp.float32)
    return (added_state, carry_decay, inject)


def compose(earlier, later):
    return (earlier[0] * later[0], later[0][:, None, None] * earlier[1] + later[1])


def on_device(
    activations, cotangent, b_proj, c_proj, dt_raw, resets, agents, agent_bias, a_log, d_skip
):
    head_count = dt_raw.shape[0]
    head_width = activations.shape[1] // head_count
    states = b_proj.shape[1]
    token_count = activations.shape[0]
    agent_ids = jnp.arange(agent_bias.shape[1])
    matches = agents[None, None, :] == agent_ids[None, :, None]
    bias_rates = jnp.sum(jnp.where(matches, agent_bias[:, :, None], 0.0), axis=1)
    rate = jnp.exp(a_log)
    b_full = b_proj.astype(jnp.float32)
    c_full = c_proj.astype(jnp.float32)
    zero_state = jnp.zeros((head_count, head_width, states), jnp.float32)
    pieces = block_pieces(activations, b_full, c_full, dt_raw, bias_rates, resets)
    cot_blocks = cotangent.reshape(token_count // BLOCK, BLOCK, -1)
    added_all, decay_all, inject_all = lax.map(
        partial(block_summary, rate=rate), pieces + (cot_blocks,)
    )

    def forward_state(state, item):
        return (item[0][:, None, None] * state + item[1], None)

    def backward_state(grad, item):
        return (item[0][:, None, None] * grad + item[1], None)

    local_state = lax.scan(forward_state, zero_state, (decay_all, added_all))[0]
    back_state = lax.scan(backward_state, zero_state, (decay_all, inject_all), reverse=True)[0]
    step_size = jax.nn.softplus(dt_raw + bias_rates)
    no_reset = (jnp.sum(resets) == 0).astype(jnp.float32)
    total_decay = jnp.exp(-rate * jnp.sum(step_size, axis=1)) * no_reset
    identity = (jnp.ones((head_count,), jnp.float32), jnp.zeros_like(zero_state))
    entry_state = entering((total_decay, local_state), ("seq", "rep"), compose, identity, False)[1]
    exit_grad = entering((total_decay, back_state), ("seq", "rep"), compose, identity, True)[1]

    def full_layer(x_in, b_part, c_part, raw_rates):
        return run_blocks(
            x_in, b_part, c_part, raw_rates, bias_rates, resets, rate, d_skip, entry_state
        )

    _, pull_all = jax.vjp(full_layer, activations, b_full, c_full, dt_raw)
    grad_input, grad_b_part, grad_c_part, grad_rate = pull_all((cotangent, exit_grad))
    grad_b, grad_c = lax.psum((grad_b_part, grad_c_part), "head")
    return (grad_input, grad_b, grad_c, grad_rate)


def solution(mesh):
    return jax.shard_map(
        on_device,
        mesh=mesh,
        in_specs=(
            P(("grp", "seq", "rep"), "head"),
            P(("grp", "seq", "rep"), "head"),
            P(("grp", "seq", "rep"), None),
            P(("grp", "seq", "rep"), None),
            P("head", ("grp", "seq", "rep")),
            P(("grp", "seq", "rep")),
            P(("grp", "seq", "rep")),
            P("head", None),
            P("head"),
            P("head"),
        ),
        out_specs=(
            P(("grp", "seq", "rep"), "head"),
            P(("grp", "seq", "rep"), None),
            P(("grp", "seq", "rep"), None),
            P("head", ("grp", "seq", "rep")),
        ),
        check_vma=False,
    )
```

profile of v0, /device:TPU:0, one launch (start us, length us, event | category | flops | bytes accessed | tf_op | source)
XLA Modules:
  0.0 532.1 jit_solution(14972050398913285322)
XLA Ops:
  15.7 6.2 %copy.230 = bf16[4,256,2048]{1,2,0:T(8,128)(2,1)} copy(bf16[4,256,2048]{2,1,0:T(8,128)(2,1)} %bitcast.526) | data formatting | bytes 8388608 | tf_op jit(solution)/shard_map/while | solution.py:131
  21.9 6.3 %copy.233 = bf16[4,256,2048]{1,2,0:T(8,128)(2,1)} copy(bf16[4,256,2048]{2,1,0:T(8,128)(2,1)} %bitcast.527) | data formatting | bytes 8388608 | tf_op jit(solution)/shard_map/while | solution.py:131
  30.4 2.5 broadcast.780.clone
  33.0 2.4 broadcast.780.clone.1
  35.4 40.7 %while.162 = (s32[]{:T(128)}, f32[4,16,128,128]{3,2,1,0:T(8,128)}, f32[4,16]{1,0:T(4,128)S(1)}, f32[4,16,128,128]{3,2,1,0:T(8,128)}, bf16[4,256,2048]{1,2,0:T(8,...) while((s32[]{:T(128)}, f32[4,16,128,128]{3,2,1,0:T(8,128)}, ...), condition=%wide.region_8.9_spmd, body=%wide.region_3.8_spmd.sunk | while | flops 271692864 | bytes 9467659 | solution.py:131
  41.8 1.9 fusion.181
  52.0 1.9 fusion.181
  62.2 1.8 fusion.181
  72.4 1.8 fusion.181
  76.1 5.8 %while.167 = (s32[]{:T(128)}, f32[16,128,128]{2,1,0:T(8,128)S(1)}, f32[4,16]{1,0:T(4,128)S(1)}, f32[4,16,128,128]{3,2,1,0:T(8,128)}, s32[]{:T(128)}, /*index=5*/s32[]{:T(128)}) while((s32[]{:T(128)}, f32[16,128,128]{2,1,0:T(8,128)S(1)}, f32[4,16]{1,0:T(4,128)S(1)}, f32[4,16,128,128]{3,2,1,0:T(8,128)}, s32[]{:T(128)}, ...), condition=%wide.region_14.15_spmd.clone, body=%wide.region_13.14_spmd.clone.sunk | while | flops 786435 | bytes 3146007 | solution.py:141
  83.0 5.8 %while.165 = (s32[]{:T(128)}, f32[16,128,128]{2,1,0:T(8,128)S(1)}, f32[4,16]{1,0:T(4,128)S(1)}, f32[4,16,128,128]{3,2,1,0:T(8,128)}, s32[]{:T(128)}, /*index=5*/s32[]{:T(128)}, s32[]{:T(128)}) while((s32[]{:T(128)}, f32[16,128,128]{2,1,0:T(8,128)S(1)}, f32[4,16]{1,0:T(4,128)S(1)}, f32[4,16,128,128]{3,2,1,0:T(8,128)}, s32[]{:T(128)}, ...), condition=%wide.region_10.11_spmd.clone, body=%wide.region_9.10_spmd.clone.sunk | while | flops 786436 | bytes 3146027 | solution.py:142
  90.0 18.9 %all-reduce.2 = f32[128]{0:T(128)S(1)} all-reduce(f32[128]{0:T(128)S(1)} %get-tuple-element.2690), channel_id=2, replica_groups=mesh['grp'=2,'seq'=4,'head'=2,'rep'=2] {'seq','rep'}, use_global_device_ids=true, to_apply=%add.2 | all-reduce | flops 128 | bytes 1024
  109.0 59.0 %all-gather.8.cloned.1.call-done = f32[128,128,128]{2,1,0:T(8,128)} async-done(((f32[16,128,128]{2,1,0:T(8,128)}), f32[128,128,128]{2,1,0:T(8,128)}) %all-gather.8.cloned.1.call-update) | async-done | bytes 8388624 | tf_op jit(solution)/shard_map/all_gather | solution.py:13
  168.0 10.7 %while.168 = (s32[]{:T(128)}, f32[16,128,128]{2,1,0:T(8,128)S(1)}, s32[]{:T(128)}, f32[8,16]{1,0:T(8,128)S(1)}, f32[8,16,128,128]{3,2,1,0:T(8,128)}, /*index=5*/s32[]{:T(128)}, s32[]{:T(128)}) while((s32[]{:T(128)}, f32[16,128,128]{2,1,0:T(8,128)S(1)}, s32[]{:T(128)}, f32[8,16]{1,0:T(8,128)S(1)}, ...), condition=%wide.region_16.17_spmd.clone, body=%wide.region_15.16_spmd.clone.sunk | while | flops 1048580 | bytes 3146025 | solution.py:25
  178.7 2.5 broadcast.780
  183.7 125.4 %while.164 = (s32[]{:T(128)}, f32[16,128,128]{2,1,0:T(8,128)S(1)}, f32[4,16,256]{2,1,0:T(8,128)S(1)}, pred[4,16,256,256]{3,2,1,0:T(32,128)(4,1)}, f32[4,16,256,2...) while((s32[]{:T(128)}, f32[16,128,128]{2,1,0:T(8,128)S(1)}, ...), condition=%wide.region_22.23_spmd.clone, body=%wide.region_17.22_spmd.clone.sunk | while | flops 250280272 | bytes 32884656 | solution.py:84
  186.0 2.0 bitcast_dynamic-update-slice_fusion.11
  188.0 5.2 fusion.215
  195.2 2.3 fusion.217
  199.4 2.7 fusion.219
  217.3 2.1 bitcast_dynamic-update-slice_fusion.11
  219.4 5.2 fusion.215
  226.6 2.2 fusion.217
  230.7 2.7 fusion.219
  248.7 2.1 bitcast_dynamic-update-slice_fusion.11
  250.7 5.2 fusion.215
  258.0 2.3 fusion.217
  262.2 2.7 fusion.219
  280.1 2.1 bitcast_dynamic-update-slice_fusion.11
  282.2 5.2 fusion.215
  289.4 2.2 fusion.217
  293.5 2.6 fusion.219
  309.0 7.7 %rev.7 = f32[8,16,128,128]{3,2,1,0:T(8,128)} reverse(f32[8,16,128,128]{3,2,1,0:T(8,128)} %bitcast.525), dimensions={0} | reverse | bytes 16777216 | tf_op jit(solution)/shard_map/rev | solution.py:15
  316.7 10.4 %while.166 = (s32[]{:T(128)}, f32[16,128,128]{2,1,0:T(8,128)S(1)}, s32[]{:T(128)}, f32[8,16]{1,0:T(8,128)S(1)}, f32[8,16,128,128]{3,2,1,0:T(8,128)}, /*index=5*/s32[]{:T(128)}, s32[]{:T(128)}) while((s32[]{:T(128)}, f32[16,128,128]{2,1,0:T(8,128)S(1)}, s32[]{:T(128)}, f32[8,16]{1,0:T(8,128)S(1)}, ...), condition=%wide.region_12.13_spmd.clone, body=%wide.region_11.12_spmd.clone.sunk | while | flops 1048580 | bytes 3146025 | solution.py:25
  327.2 2.5 broadcast_in_dim.286.clone
  332.0 150.9 %while.163 = (s32[]{:T(128)}, f32[16,128,128]{2,1,0:T(8,128)S(1)}, bf16[4,256,2048]{2,1,0:T(8,128)(2,1)}, f32[4,256,128]{2,1,0:T(8,128)}, f32[4,256,128]{2,1,0:T...) while((s32[]{:T(128)}, f32[16,128,128]{2,1,0:T(8,128)S(1)}, ...), condition=%wide.region_36.37_spmd, body=%wide.region_23.36_spmd.sunk | while | flops 1299697664 | bytes 46902400 | solution.py:84
  342.4 6.6 %fusion.200 = (f32[16,256]{1,0:T(8,128)S(1)}, f32[16,256]{1,0:T(8,128)S(1)}, f32[256,256]{1,0:T(8,128)S(1)}, f32[16,256]{1,0:T(8,128)S(1)}) fusion(f32[4,16,256,256]{3,2,1,0:T(8,128)} %get-tuple-element.3788, s32[]{:T(128)S(6)} %sub.214, f32[16,256]{1,0:T(8,128)S(1)} %dynamic-slice_bitcast_fusion.28, ...), kind=kOutput, calls=%fused_computation.101.clone.1 | convolution fusion | flops 281989120 | bytes 16319488 | tf_op jit(solution)/shard_map/transpose(jvp())/while/body/eval_jaxpr/hij,jhp->ihp/dot_general | solution.py:46
  352.0 2.5 reduce-window.104
  356.2 1.9 fusion.203
  358.3 2.2 fusion.201
  360.4 2.0 fusion.197
  362.5 2.9 fusion.198
  367.9 1.8 fusion.196
  380.1 6.6 %fusion.200 = (f32[16,256]{1,0:T(8,128)S(1)}, f32[16,256]{1,0:T(8,128)S(1)}, f32[256,256]{1,0:T(8,128)S(1)}, f32[16,256]{1,0:T(8,128)S(1)}) fusion(f32[4,16,256,256]{3,2,1,0:T(8,128)} %get-tuple-element.3788, s32[]{:T(128)S(6)} %sub.214, f32[16,256]{1,0:T(8,128)S(1)} %dynamic-slice_bitcast_fusion.28, ...), kind=kOutput, calls=%fused_computation.101.clone.1 | convolution fusion | flops 281989120 | bytes 16319488 | tf_op jit(solution)/shard_map/transpose(jvp())/while/body/eval_jaxpr/hij,jhp->ihp/dot_general | solution.py:46
  389.7 2.5 reduce-window.104
  394.0 1.9 fusion.203
  396.0 2.2 fusion.201
  398.2 2.0 fusion.197
  400.2 2.9 fusion.198
  417.8 6.6 %fusion.200 = (f32[16,256]{1,0:T(8,128)S(1)}, f32[16,256]{1,0:T(8,128)S(1)}, f32[256,256]{1,0:T(8,128)S(1)}, f32[16,256]{1,0:T(8,128)S(1)}) fusion(f32[4,16,256,256]{3,2,1,0:T(8,128)} %get-tuple-element.3788, s32[]{:T(128)S(6)} %sub.214, f32[16,256]{1,0:T(8,128)S(1)} %dynamic-slice_bitcast_fusion.28, ...), kind=kOutput, calls=%fused_computation.101.clone.1 | convolution fusion | flops 281989120 | bytes 16319488 | tf_op jit(solution)/shard_map/transpose(jvp())/while/body/eval_jaxpr/hij,jhp->ihp/dot_general | solution.py:46
  427.5 2.5 reduce-window.104
  431.7 1.9 fusion.203
  433.7 2.2 fusion.201
  435.9 2.0 fusion.197
  437.9 2.9 fusion.198
  455.6 6.6 %fusion.200 = (f32[16,256]{1,0:T(8,128)S(1)}, f32[16,256]{1,0:T(8,128)S(1)}, f32[256,256]{1,0:T(8,128)S(1)}, f32[16,256]{1,0:T(8,128)S(1)}) fusion(f32[4,16,256,256]{3,2,1,0:T(8,128)} %get-tuple-element.3788, s32[]{:T(128)S(6)} %sub.214, f32[16,256]{1,0:T(8,128)S(1)} %dynamic-slice_bitcast_fusion.28, ...), kind=kOutput, calls=%fused_computation.101.clone.1 | convolution fusion | flops 281989120 | bytes 16319488 | tf_op jit(solution)/shard_map/transpose(jvp())/while/body/eval_jaxpr/hij,jhp->ihp/dot_general | solution.py:46
  465.2 2.5 reduce-window.104
  469.4 1.9 fusion.203
  471.5 2.2 fusion.201
  473.6 2.0 fusion.197
  475.7 2.9 fusion.198
  484.4 37.4 %all-reduce.6.cloned.1.call-done = (f32[1024,128]{1,0:T(8,128)}, f32[1024,128]{1,0:T(8,128)}) async-done(((f32[1024,128]{1,0:T(8,128)}, f32[1024,128]{1,0:T(8,128)}), (f32[1024,128]{1,0:T(8,128)}, f32[1024,128]{1,0:T(8,128)})) %all-reduce.6.cloned.1.call-update) | async-done | bytes 1048592 | tf_op jit(solution)/shard_map/psum | solution.py:157
  521.8 1.9 copy.502
  523.7 1.9 copy.503
  (525 shorter events, 230.7 us)
Async XLA Ops:
  7.2 160.8 %all-gather.8.cloned.1.call-start = ((), (), s32[]{:S(2)}) async-start(), calls=%async_computation.1 | async-start | bytes 9437184 | tf_op jit(solution)/shard_map/all_gather | solution.py:13
  21.9 6.3 %copy-start.2 = (bf16[1024,128]{1,0:T(8,128)(2,1)S(1)}, bf16[1024,128]{1,0:T(8,128)(2,1)}, u32[]{:S(2)}) copy-start(bf16[1024,128]{1,0:T(8,128)(2,1)} %param.26) | copy-start | bytes 786436
  21.9 7.1 %copy-start.5 = (u32[32]{0:T(128)S(1)}, u32[32]{0:T(128)}, u32[]{:S(2)}) copy-start(u32[32]{0:T(128)} %constant.361) | copy-start | bytes 388
  21.9 8.4 %copy-start.4 = (f32[16]{0:T(128)S(1)}, f32[16]{0:T(128)}, u32[]{:S(2)}) copy-start(f32[16]{0:T(128)} %param.32) | copy-start | bytes 196
  81.9 1.0 copy-start
  82.9 226.1 %all-gather.6.cloned.1.call-start = ((), (), s32[]{:S(2)}) async-start(), calls=%async_computation | async-start | bytes 9437184 | tf_op jit(solution)/shard_map/all_gather | solution.py:13
  88.8 1.0 copy-start.1
  89.8 432.0 %all-reduce.6.cloned.1.call-start = ((), (), s32[]{:S(2)}) async-start(), calls=%async_computation.2 | async-start | bytes 2097152 | tf_op jit(solution)/shard_map/psum | solution.py:157
  327.2 4.8 copy-start.3
Sparse Core Ops, SparseCore 0:
  83.0 84.9 all-gather.7
  170.2 80.5 all-gather.5
  483.1 38.7 all-reduce.5
where the time goes:
time: 537 us; the launch traced here: 532 us
  local copies, waits for them, and re-layouts  146 us (27%)
  other arithmetic  138 us (26%)
  matrix products  111 us (21%)
  waiting for transfers between devices  96.4 us (18%)
  blocking collectives  18.9 us (4%)
  between operations  15.4 us (3%)
  loops' own time  6.56 us (1%)
    dynamic_update_slice x36, other arithmetic, run_blocks(): lax.scan(partial(block_terms, rate=rate, d_skip=d_skip), carried, pieces)  60.2 us
    all_gather x2, waiting for transfers between devices, entering(): pieces = jax.tree.map(lambda part: lax.all_gather(part, axis), value)  59 us
    psum x1, waiting for transfers between devices, on_device(): grad_b, grad_c = lax.psum((grad_b_part, grad_c_part), 'head')  37.4 us
    dot_general x8, matrix products, block_terms(): jnp.einsum('hij,jhp->ihp', mixing, x_heads, preferred_element_type=jnp.fl...  34.6 us
    dynamic_update_slice x36, local copies, waits for them, and re-layouts, run_blocks(): lax.scan(partial(block_terms, rate=rate, d_skip=d_skip), carried, pieces)  33.4 us
    dot_general x12, matrix products, block_terms(): jnp.dot(c_blk, b_blk.T, precision=lax.Precision.HIGHEST, preferred_elemen...  24.7 us
    dynamic_slice x40, local copies, waits for them, and re-layouts, on_device(): lax.map(partial(block_summary, rate=rate), pieces + (cot_blocks,))  24.2 us
    dot_general x12, matrix products, block_terms(): jnp.einsum('jhp,hjn->hpn', x_heads, b_scaled, preferred_element_type=jnp....  22.9 us
  transfers between devices with their start and end apart: 3, of which 2 were waited for; matrix products, arithmetic and copies ran while one was open for 27% of the time, Pallas kernels for 0%

commit v1 on v0

v1 whole, which is shorter than its diff:
```python
from functools import partial

import jax
import jax.numpy as jnp
from jax import lax
from jax.experimental import pallas as pl
from jax.experimental.pallas import tpu as pltpu
from jax.sharding import PartitionSpec as P

BLOCK = 256
LOG2E = 1.4426950408889634
HI = lax.Precision.HIGHEST
F32 = jnp.float32
BF16 = jnp.bfloat16
NT = (((1,), (1,)), ((), ()))
VMEM_LIMIT = 50 * 1024 * 1024


def dot(a, b):
    return jnp.dot(a, b, preferred_element_type=F32)


def dot_nt(a, b):
    return lax.dot_general(a, b, NT, preferred_element_type=F32)


def dot_hi(a, b):
    return jnp.dot(a, b, precision=HI, preferred_element_type=F32)


def iota(shape, axis):
    return lax.broadcasted_iota(jnp.int32, shape, axis)


def summary_kernel(
    nb, x_ref, dy_ref, b_ref, c_ref, raw_ref, res_ref, ag_ref, bias_ref, alog_ref,
    rows_ref, aux_ref, added_ref, inject_ref, local_ref, back_ref, gam_ref, bt_s, ct_s,
):
    h = pl.program_id(0)
    heads = raw_ref.shape[0]

    @pl.when(h == 0)
    def _():
        upper = (iota((BLOCK, BLOCK), 0) <= iota((BLOCK, BLOCK), 1)).astype(F32)
        rate = jnp.exp(alog_ref[...])
        for b in range(nb):
            sl = slice(b * BLOCK, (b + 1) * BLOCK)
            bt_s[:, sl] = b_ref[sl, :].astype(F32).T
            ct_s[:, sl] = c_ref[sl, :].astype(F32).T
            onehot = (ag_ref[:, sl] == iota((bias_ref.shape[1], BLOCK), 0)).astype(F32)
            v = raw_ref[:, sl] + dot_hi(bias_ref[...], onehot)
            ev = jnp.exp(v)
            s = jnp.where(v > 15.0, v, jnp.log1p(ev))
            log_decay = -rate * s
            cum = dot_hi(log_decay, upper)
            res = jnp.broadcast_to(res_ref[:, sl].astype(F32), (8, BLOCK))
            ep = dot_hi(res, upper)[:1]
            cum2 = cum * LOG2E
            entry = jnp.where(ep < 0.5, jnp.exp(cum), 0.0)
            last = cum[:, BLOCK - 1 :]
            to_end = jnp.where(jnp.abs(ep - ep[:, BLOCK - 1 :]) < 0.5, jnp.exp(last - cum) * s, 0.0)
            rows_ref[:, b, :] = cum2
            rows_ref[:, nb + b, :] = cum2 - jnp.log2(s)
            rows_ref[:, 2 * nb + b, :] = entry
            rows_ref[:, 3 * nb + b, :] = to_end
            aux_ref[0, :, sl] = 1.0 / s
            aux_ref[1, :, sl] = ev / (1.0 + ev)
            aux_ref[2, :, sl] = jnp.broadcast_to(ep, (heads, BLOCK))

    added, inject, gammas = [], [], []
    for b in range(nb):
        sl = slice(b * BLOCK, (b + 1) * BLOCK)
        e_row = rows_ref[h, pl.ds(2 * nb + b, 1), :]
        t_row = rows_ref[h, pl.ds(3 * nb + b, 1), :]
        add = dot((bt_s[:, sl] * t_row).astype(BF16), x_ref[sl, :])
        inj = dot((ct_s[:, sl] * e_row).astype(BF16), dy_ref[sl, :]).astype(BF16)
        added_ref[0, b] = add
        inject_ref[0, b] = inj
        added.append(add)
        inject.append(inj.astype(F32))
        gammas.append(e_row[:, BLOCK - 1 :])
    local, back, total = added[0], inject[nb - 1], gammas[0]
    for b in range(1, nb):
        local = gammas[b] * local + added[b]
        total = total * gammas[b]
        back = gammas[nb - 1 - b] * back + inject[nb - 1 - b]
    local_ref[0] = local
    back_ref[0] = back
    gam_ref[0] = jnp.broadcast_to(total, gam_ref.shape[1:])


def grad_kernel(
    nb, x_ref, dy_ref, b_ref, c_ref, rows_ref, aux_ref, added_ref, inject_ref,
    entry_ref, exit_ref, alog_ref, dskip_ref,
    gx_ref, gb_ref, gc_ref, gr_ref,
    bt_s, ct_s, st_s, ds_s, dbt_s, dct_s, drow_s, dcol_s,
):
    h = pl.program_id(0)

    @pl.when(h == 0)
    def _():
        for b in range(nb):
            sl = slice(b * BLOCK, (b + 1) * BLOCK)
            bt_s[:, sl] = b_ref[sl, :].astype(F32).T
            ct_s[:, sl] = c_ref[sl, :].astype(F32).T
            ep = aux_ref[2, :8, sl]
            ep_col = ep.T[:, :1]
            mask = (iota((BLOCK, BLOCK), 0) <= iota((BLOCK, BLOCK), 1)) & (
                jnp.abs(ep_col - ep[:1]) < 0.5
            )
            st_s[b] = jnp.where(mask, dot_nt(b_ref[sl, :], c_ref[sl, :]), 0.0)
        ds_s[...] = jnp.zeros_like(ds_s)
        dbt_s[...] = jnp.zeros_like(dbt_s)
        dct_s[...] = jnp.zeros_like(dct_s)

    rows = rows_ref[0]
    cols = rows.T
    ones = jnp.ones((8, x_ref.shape[1]), BF16)
    d_h = dskip_ref[h]
    gam = [rows[2 * nb + b : 2 * nb + b + 1, BLOCK - 1 :] for b in range(nb)]
    states = [entry_ref[0]]
    for b in range(nb):
        states.append(gam[b] * states[b] + added_ref[0, b])
    grads = [exit_ref[0]]
    for b in range(nb - 1, 0, -1):
        grads.insert(0, gam[b] * grads[0] + inject_ref[0, b].astype(F32))
    for b in range(nb):
        sl = slice(b * BLOCK, (b + 1) * BLOCK)
        x, dy = x_ref[sl, :], dy_ref[sl, :]
        g16 = grads[b].astype(BF16)
        s16 = states[b].astype(BF16)
        dmt = dot_nt(x, dy)
        decay = jnp.exp2(rows[b : b + 1] - cols[:, nb + b : nb + b + 1])
        mt = st_s[b] * decay
        ds_s[b] += dmt * decay
        row = jnp.sum(dmt * mt, axis=0, keepdims=True)
        dcs = dot_nt(s16, dy) * rows[2 * nb + b : 2 * nb + b + 1]
        dct_s[:, sl] += dcs
        row += jnp.sum(dcs * ct_s[:, sl], axis=0, keepdims=True)
        row_end = jnp.sum(jnp.sum(grads[b] * states[b + 1], axis=0, keepdims=True), axis=1, keepdims=True)
        dbt_s[:, sl] += dot_nt(g16, x) * rows[3 * nb + b : 3 * nb + b + 1]
        dx = dot(mt.astype(BF16), dy) + cols[:, 3 * nb + b : 3 * nb + b + 1] * dot(b_ref[sl, :], g16)
        z = x.astype(F32) * dx
        zh = z.astype(BF16)
        zl = (z - zh.astype(F32)).astype(BF16)
        col = (dot_nt(ones, zh) + dot_nt(ones, zl))[:1]
        gx_ref[sl, :] = (dx + d_h * dy.astype(F32)).astype(BF16)
        last = iota((1, BLOCK), 1) == BLOCK - 1
        drow_s[pl.ds(h, 1), sl] = row - col + jnp.where(last, row_end, 0.0)
        dcol_s[pl.ds(h, 1), sl] = col

    @pl.when(h == pl.num_programs(0) - 1)
    def _():
        lower = (iota((BLOCK, BLOCK), 0) >= iota((BLOCK, BLOCK), 1)).astype(F32)
        rate = jnp.exp(alog_ref[...])
        for b in range(nb):
            sl = slice(b * BLOCK, (b + 1) * BLOCK)
            dlog = dot_hi(drow_s[:, sl], lower)
            gr_ref[:, sl] = (dcol_s[:, sl] * aux_ref[0, :, sl] - rate * dlog) * aux_ref[1, :, sl]
            ep = aux_ref[2, :8, sl]
            ep_col = ep.T[:, :1]
            mask = (iota((BLOCK, BLOCK), 0) <= iota((BLOCK, BLOCK), 1)) & (
                jnp.abs(ep_col - ep[:1]) < 0.5
            )
            ds = jnp.where(mask, ds_s[b], 0.0)
            dh = ds.astype(BF16)
            dl = (ds - dh.astype(F32)).astype(BF16)
            ct = ct_s[:, sl].astype(BF16)
            bt = bt_s[:, sl].astype(BF16)
            gb_ref[sl, :] = (dbt_s[:, sl] + dot_nt(ct, dh) + dot_nt(ct, dl)).T
            gc_ref[sl, :] = (dct_s[:, sl] + dot(bt, dh) + dot(bt, dl)).T


def whole(shape):
    return pl.BlockSpec(shape, lambda h: (0,) * len(shape))


def per_head(shape):
    return pl.BlockSpec((1,) + shape, lambda h: (h,) + (0,) * len(shape))


def entering(value, axis, backward):
    count, mine = (lax.axis_size(axis), lax.axis_index(axis))
    decay, state = jax.tree.map(lambda part: lax.all_gather(part, axis), value)
    if backward:
        decay, state = decay[::-1], state[::-1]
        mine = count - 1 - mine
    total = jnp.zeros_like(value[1])
    for k in range(count - 1):
        longer = decay[k][:, :1] * total + state[k]
        total = jnp.where(k < mine, longer, total)
    return total


def on_device(
    activations, cotangent, b_proj, c_proj, dt_raw, resets, agents, agent_bias, a_log, d_skip
):
    heads = dt_raw.shape[0]
    width = activations.shape[1] // heads
    n = b_proj.shape[1]
    tokens = activations.shape[0]
    nb = tokens // BLOCK
    xspec = pl.BlockSpec((tokens, width), lambda h: (0, h))
    alog = a_log[:, None]
    sds = jax.ShapeDtypeStruct
    rows, aux, added, inject, local, back, gam = pl.pallas_call(
        partial(summary_kernel, nb),
        grid=(heads,),
        in_specs=[
            xspec, xspec, whole((tokens, n)), whole((tokens, n)), whole((heads, tokens)),
            whole((1, tokens)), whole((1, tokens)), whole(agent_bias.shape), whole((heads, 1)),
        ],
        out_specs=[
            whole((heads, 4 * nb, BLOCK)), whole((3, heads, tokens)), per_head((nb, n, width)),
            per_head((nb, n, width)), per_head((n, width)), per_head((n, width)), per_head((8, width)),
        ],
        out_shape=[
            sds((heads, 4 * nb, BLOCK), F32), sds((3, heads, tokens), F32),
            sds((heads, nb, n, width), F32), sds((heads, nb, n, width), BF16),
            sds((heads, n, width), F32), sds((heads, n, width), F32), sds((heads, 8, width), F32),
        ],
        scratch_shapes=[pltpu.VMEM((n, tokens), F32), pltpu.VMEM((n, tokens), F32)],
        compiler_params=pltpu.CompilerParams(vmem_limit_bytes=VMEM_LIMIT),
    )(
        activations, cotangent, b_proj, c_proj, dt_raw, resets[None], agents[None], agent_bias, alog
    )
    entry = entering((gam, local), ("seq", "rep"), False)
    exit_grad = entering((gam, back), ("seq", "rep"), True)
    grad_x, grad_b, grad_c, grad_rate = pl.pallas_call(
        partial(grad_kernel, nb),
        grid=(heads,),
        in_specs=[
            xspec, xspec, whole((tokens, n)), whole((tokens, n)), per_head((4 * nb, BLOCK)),
            whole((3, heads, tokens)), per_head((nb, n, width)), per_head((nb, n, width)),
            per_head((n, width)), per_head((n, width)), whole((heads, 1)),
            pl.BlockSpec(memory_space=pltpu.SMEM),
        ],
        out_specs=[xspec, whole((tokens, n)), whole((tokens, n)), whole((heads, tokens))],
        out_shape=[
            sds(activations.shape, BF16), sds((tokens, n), F32), sds((tokens, n), F32),
            sds((heads, tokens), F32),
        ],
        scratch_shapes=[
            pltpu.VMEM((n, tokens), F32), pltpu.VMEM((n, tokens), F32),
            pltpu.VMEM((nb, BLOCK, BLOCK), F32), pltpu.VMEM((nb, BLOCK, BLOCK), F32),
            pltpu.VMEM((n, tokens), F32), pltpu.VMEM((n, tokens), F32),
            pltpu.VMEM((heads, tokens), F32), pltpu.VMEM((heads, tokens), F32),
        ],
        compiler_params=pltpu.CompilerParams(vmem_limit_bytes=VMEM_LIMIT),
    )(
        activations, cotangent, b_proj, c_proj, rows, aux, added, inject, entry, exit_grad, alog,
        d_skip,
    )
    grad_b, grad_c = lax.psum((grad_b, grad_c), "head")
    return (grad_x, grad_b, grad_c, grad_rate)


def solution(mesh):
    tok = ("grp", "seq", "rep")
    return jax.shard_map(
        on_device,
        mesh=mesh,
        in_specs=(
            P(tok, "head"), P(tok, "head"), P(tok, None), P(tok, None), P("head", tok),
            P(tok), P(tok), P("head", None), P("head"), P("head"),
        ),
        out_specs=(P(tok, "head"), P(tok, None), P(tok, None), P("head", tok)),
        check_vma=False,
    )
```

time: 537 us -> 282 us (0.53)
  local copies, waits for them, and re-layouts: 146 us -> 9.29 us
  other arithmetic: 138 us -> 9.35 us
  matrix products: 111 us -> 0 us
  waiting for transfers between devices: 96.4 us -> 186 us
  Pallas kernels: 0 us -> 46 us
  loops' own time: 6.56 us -> 0 us
    dot_general x48 -> x0, matrix products: 111 us -> none  [the longest x8 34.6 us: block_terms(): jnp.einsum('hij,jhp->ihp', mixing, x_heads, preferred_element_type=jnp.fl...]
    all_gather x2, waiting for transfers between devices: 59 us -> 146 us  [entering(): decay, state = jax.tree.map(lambda part: lax.all_gather(part, axis), value)]
    dynamic_update_slice x36 -> x0, other arithmetic: 60.2 us -> none  [run_blocks(): lax.scan(partial(block_terms, rate=rate, d_skip=d_skip), carried, pieces)]
    pallas_call x0 -> x2, Pallas kernels: none -> 46 us  [the longest x1 30.6 us: on_device(): pl.pallas_call(partial(grad_kernel, nb), grid=(heads,), in_specs=[xspec,...]
    dynamic_update_slice x48 -> x0, local copies, waits for them, and re-layouts: 37.9 us -> none  [the longest x36 33.4 us: run_blocks(): lax.scan(partial(block_terms, rate=rate, d_skip=d_skip), carried, pieces)]
    dynamic_slice x60 -> x0, local copies, waits for them, and re-layouts: 31.3 us -> none  [the longest x40 24.2 us: on_device(): lax.map(partial(block_summary, rate=rate), pieces + (cot_blocks,))]
    another operation x69 -> x0, other arithmetic: 19 us -> none
    unnamed x1 -> x0, blocking collectives: 18.9 us -> none
  transfers between devices with their start and end apart: 3 -> 3, of which waited for: 2 -> 3; matrix products, arithmetic and copies ran while one was open for 27% -> 1% of each run, Pallas kernels for 0% -> 0%
where the time goes in v1:
time: 282 us; the launch traced here: 281 us
  waiting for transfers between devices  186 us (66%)
  Pallas kernels  46 us (16%)
  blocking collectives  17.2 us (6%)
  between operations  13.8 us (5%)
  other arithmetic  9.35 us (3%)
  local copies, waits for them, and re-layouts  9.29 us (3%)
    all_gather x2, waiting for transfers between devices, entering(): decay, state = jax.tree.map(lambda part: lax.all_gather(part, axis), value)  146 us
    psum x1, waiting for transfers between devices, on_device(): grad_b, grad_c = lax.psum((grad_b, grad_c), 'head')  38.9 us
    pallas_call x1, Pallas kernels, on_device(): pl.pallas_call(partial(grad_kernel, nb), grid=(heads,), in_specs=[xspec,...  30.6 us
    all_gather x1, blocking collectives, entering(): decay, state = jax.tree.map(lambda part: lax.all_gather(part, axis), value)  17.2 us
    pallas_call x1, Pallas kernels, on_device(): pl.pallas_call(partial(summary_kernel, nb), grid=(heads,), in_specs=[xspe...  15.4 us
    select_n x2, other arithmetic, entering(): total = jnp.where(k < mine, longer, total)  9.31 us
    unnamed x20, local copies, waits for them, and re-layouts  8.55 us
  transfers between devices with their start and end apart: 3, of which 3 were waited for; matrix products, arithmetic and copies ran while one was open for 1% of the time, Pallas kernels for 0%

profile of v1, /device:TPU:0, one launch (start us, length us, event | category | flops | bytes accessed | tf_op | source)
XLA Modules:
  0.0 281.3 jit_solution(9897685074032420125)
XLA Ops:
  7.2 0.0 all-gather.6.cloned.1.call-start
  7.2 0.7 copy.16.alog_ref
  7.9 0.0 copy-start
  7.9 0.9 copy-done
  8.9 0.0 copy-start.2
  8.9 0.9 copy-done.2
  9.8 0.0 copy-start.4
  9.8 0.8 copy-done.4
  10.7 0.0 copy-start.5
  10.7 0.7 copy-done.5
  11.4 0.0 copy-start.6
  11.4 0.7 copy-done.6
  12.1 0.0 copy-start.7
  12.1 0.7 copy-done.7
  12.8 15.4 %shard_map.129 = (f32[16,16,256]{2,1,0:T(8,128)S(1)}, f32[3,16,1024]{2,1,0:T(8,128)S(1)}, f32[16,4,128,128]{3,2,1,0:T(8,128)}, bf16[16,4,128,128]{3,2,1,0:T(8,12...) custom-call(bf16[1024,2048]{1,0:T(8,128)(2,1)} %x_ref.3, ...), custom_call_target="tpu_custom_call" | custom-call | tf_op jit(solution)/shard_map/pallas_call | solution.py:206
  28.2 0.0 all-gather.6.cloned.1.call-update
  28.2 0.0 all-gather.8.cloned.1.call-start
  28.3 0.7 all-gather.8.cloned.1.call-update
  29.0 0.0 all-reduce.3.cloned.1.call-start
  29.0 17.2 %all-gather = f32[128,8,128]{2,1,0:T(8,128)S(1)} all-gather(f32[16,8,128]{2,1,0:T(8,128)S(1)} %get-tuple-element.19), channel_id=2, replica_groups=mesh['grp'=2,'seq'=4,'head'=2,'rep'=2] {'seq','rep'}, dimensions={0}, use_global_device_ids=true | all-gather | bytes 589824 | tf_op jit(solution)/shard_map/all_gather | solution.py:184
  46.3 67.5 %all-gather.6.cloned.1.call-done = f32[128,128,128]{2,1,0:T(8,128)} async-done(((f32[16,128,128]{2,1,0:T(8,128)}), f32[128,128,128]{2,1,0:T(8,128)}) %all-gather.6.cloned.1.call-update) | async-done | bytes 8388624 | tf_op jit(solution)/shard_map/all_gather | solution.py:184
  113.8 4.1 %fusion.7.entry_ref = f32[16,128,128]{2,1,0:T(8,128)S(1)} fusion(f32[128,128,128]{2,1,0:T(8,128)} %all-gather.6.cloned.1.call-done, f32[16,128]{1,0:T(8,128)S(1)} %bitcast.26, f32[16,128]{1,0:T(8,128)S(1)} %bitcast.13, f32[16,128]{1,0:T(8,128)S(1)} %bitcast.15, f32[16,128]{1,0:T(8,128)S(1)} %bitcast.17, f32[16,128]{1,0:T(8,128)S(1)} %bitcast.19, ...), kind=kLoop, calls=%fused_computation.15 | loop fusion | flops 5242880 | bytes 8445959 | tf_op jit(solution)/shard_map/jit(_where)/select_n | solution.py:191
  117.9 78.4 %all-gather.8.cloned.1.call-done = f32[128,128,128]{2,1,0:T(8,128)} async-done(((f32[16,128,128]{2,1,0:T(8,128)}), f32[128,128,128]{2,1,0:T(8,128)}) %all-gather.8.cloned.1.call-update) | async-done | bytes 8388624 | tf_op jit(solution)/shard_map/all_gather | solution.py:184
  196.3 0.0 copy-start.1
  196.3 0.0 copy-start.3
  196.3 0.0 copy-start.8
  196.3 5.2 %fusion.exit_ref = f32[16,128,128]{2,1,0:T(8,128)} fusion(f32[128,128,128]{2,1,0:T(8,128)} %all-gather.8.cloned.1.call-done, f32[16,128]{1,0:T(8,128)S(1)} %bitcast.25, f32[16,128]{1,0:T(8,128)S(1)} %bitcast.14, f32[16,128]{1,0:T(8,128)S(1)} %bitcast.16, f32[16,128]{1,0:T(8,128)S(1)} %bitcast.18, f32[16,128]{1,0:T(8,128)S(1)} %bitcast.20, ...), kind=kLoop, calls=%fused_computation.1 | loop fusion | flops 5242880 | bytes 8445959 | tf_op jit(solution)/shard_map/jit(_where)/select_n | solution.py:191
  201.5 0.0 copy-done.1
  201.5 0.0 copy-done.3
  201.5 0.0 copy-done.8
  201.5 30.6 %shard_map.130 = (bf16[1024,2048]{1,0:T(8,128)(2,1)}, f32[1024,128]{1,0:T(8,128)}, f32[1024,128]{1,0:T(8,128)}, f32[16,1024]{1,0:T(8,128)}) custom-call(bf16[1024,2048]{1,0:T(8,128)(2,1)} %x_ref.3, bf16[1024,2048]{1,0:T(8,128)(2,1)} %dy_ref.3, bf16[1024,128]{1,0:T(8,128)(2,1)S(1)} %copy-done.1, bf16[1024,128]{1,0:T(8,128)(2,1)S(1)} %copy-done.3, ...), custom_call_target="tpu_custom_call" | custom-call | tf_op jit(solution)/shard_map/pallas_call | solution.py:229
  232.1 0.0 all-reduce.3.cloned.1.call-update
  232.1 38.9 %all-reduce.3.cloned.1.call-done = (f32[1024,128]{1,0:T(8,128)}, f32[1024,128]{1,0:T(8,128)}) async-done(((f32[1024,128]{1,0:T(8,128)}, f32[1024,128]{1,0:T(8,128)}), (f32[1024,128]{1,0:T(8,128)}, f32[1024,128]{1,0:T(8,128)})) %all-reduce.3.cloned.1.call-update) | async-done | bytes 1048592 | tf_op jit(solution)/shard_map/psum | solution.py:254
  271.0 1.9 copy.20
  272.9 1.9 copy.21
  (1 shorter events, 0.0 us)
Async XLA Ops:
  7.2 106.7 %all-gather.6.cloned.1.call-start = ((), (), s32[]{:S(2)}) async-start(), calls=%async_computation | async-start | bytes 9437184 | tf_op jit(solution)/shard_map/all_gather | solution.py:184
  7.9 0.9 copy-start
  8.9 0.9 copy-start.2
  9.8 0.8 copy-start.4
  10.7 0.7 copy-start.5
  11.4 0.7 copy-start.6
  12.1 0.7 copy-start.7
  28.2 168.1 %all-gather.8.cloned.1.call-start = ((), (), s32[]{:S(2)}) async-start(), calls=%async_computation.1 | async-start | bytes 9437184 | tf_op jit(solution)/shard_map/all_gather | solution.py:184
  29.0 242.1 %all-reduce.3.cloned.1.call-start = ((), (), s32[]{:S(2)}) async-start(), calls=%async_computation.2 | async-start | bytes 2097152 | tf_op jit(solution)/shard_map/psum | solution.py:254
  196.3 5.2 %copy-start.1 = (bf16[1024,128]{1,0:T(8,128)(2,1)S(1)}, bf16[1024,128]{1,0:T(8,128)(2,1)}, u32[]{:S(2)}) copy-start(bf16[1024,128]{1,0:T(8,128)(2,1)} %b_ref.3) | copy-start | bytes 786436
  196.3 5.2 %copy-start.3 = (bf16[1024,128]{1,0:T(8,128)(2,1)S(1)}, bf16[1024,128]{1,0:T(8,128)(2,1)}, u32[]{:S(2)}) copy-start(bf16[1024,128]{1,0:T(8,128)(2,1)} %c_ref.3) | copy-start | bytes 786436
  196.3 5.2 %copy-start.8 = (f32[16]{0:T(128)S(1)}, f32[16]{0:T(128)}, u32[]{:S(2)}) copy-start(f32[16]{0:T(128)} %dskip_ref.1) | copy-start | bytes 196
Sparse Core Ops, SparseCore 0:
  28.3 85.4 all-gather.5
  115.4 80.7 all-gather.7
  232.2 38.7 all-reduce.2

commit v2 on v1

--- a/solution.py
+++ b/solution.py
@@ -179,17 +179,161 @@
     return pl.BlockSpec((1,) + shape, lambda h: (h,) + (0,) * len(shape))
 
 
-def entering(value, axis, backward):
-    count, mine = (lax.axis_size(axis), lax.axis_index(axis))
-    decay, state = jax.tree.map(lambda part: lax.all_gather(part, axis), value)
-    if backward:
-        decay, state = decay[::-1], state[::-1]
-        mine = count - 1 - mine
-    total = jnp.zeros_like(value[1])
-    for k in range(count - 1):
-        longer = decay[k][:, :1] * total + state[k]
-        total = jnp.where(k < mine, longer, total)
-    return total
+MESH = pl.DeviceIdType.MESH
+AHEAD = 2
+
+
+def chain_kernel(
+    gam_ref, local_ref, back_ref, entry_ref, exit_ref,
+    fin_s, fout_s, bin_s, bout_s, fsend, frecv, bsend, brecv,
+):
+    reps = lax.axis_size("rep")
+    last = lax.axis_size("seq") * reps - 1
+    mine = lax.axis_index("seq") * reps + lax.axis_index("rep")
+    steps = fsend.shape[0]
+    per = gam_ref.shape[0] // steps
+
+    def place(index):
+        return {"seq": index // reps, "rep": index % reps}
+
+    barrier = pltpu.get_barrier_semaphore()
+
+    @pl.when(mine > 0)
+    def _():
+        pl.semaphore_signal(barrier, inc=1, device_id=place(mine - 1), device_id_type=MESH)
+
+    @pl.when(mine < last)
+    def _():
+        pl.semaphore_signal(barrier, inc=1, device_id=place(mine + 1), device_id_type=MESH)
+
+    edge = (mine == 0) | (mine == last)
+
+    @pl.when(edge)
+    def _():
+        pl.semaphore_wait(barrier, 1)
+
+    @pl.when(jnp.logical_not(edge))
+    def _():
+        pl.semaphore_wait(barrier, 2)
+
+    def hop(k, out_s, in_s, send, recv, target):
+        sl = pl.ds(k * per, per)
+        return pltpu.make_async_remote_copy(
+            src_ref=out_s.at[sl], dst_ref=in_s.at[sl], send_sem=send.at[k], recv_sem=recv.at[k],
+            device_id=place(target), device_id_type=MESH,
+        )
+
+    def advance(k, first, final, target, own_ref, got_ref, out_s, in_s, send, recv):
+        sl = pl.ds(k * per, per)
+
+        @pl.when(first)
+        def _():
+            got_ref[sl] = jnp.zeros_like(got_ref[sl])
+            out_s[sl] = own_ref[sl]
+
+        @pl.when(jnp.logical_not(first))
+        def _():
+            hop(k, out_s, in_s, send, recv, target).wait_recv()
+            got = in_s[sl]
+            got_ref[sl] = got
+            out_s[sl] = gam_ref[sl, :1, :] * got + own_ref[sl]
+
+        @pl.when(jnp.logical_not(final))
+        def _():
+            hop(k, out_s, in_s, send, recv, target).start()
+
+    right = jnp.minimum(mine + 1, last)
+    left = jnp.maximum(mine - 1, 0)
+
+    def tick(t, _):
+        kf = t - mine * AHEAD
+        kb = t - (last - mine) * AHEAD
+
+        @pl.when((kf >= 0) & (kf < steps))
+        def _():
+            advance(kf, mine == 0, mine == last, right, local_ref, entry_ref, fout_s, fin_s, fsend, frecv)
+
+        @pl.when((kb >= 0) & (kb < steps))
+        def _():
+            advance(kb, mine == last, mine == 0, left, back_ref, exit_ref, bout_s, bin_s, bsend, brecv)
+
+        return 0
+
+    lax.fori_loop(0, last * AHEAD + steps, tick, 0)
+
+    def drain(k, _):
+        @pl.when(mine < last)
+        def _():
+            hop(k, fout_s, fin_s, fsend, frecv, right).wait_send()
+
+        @pl.when(mine > 0)
+        def _():
+            hop(k, bout_s, bin_s, bsend, brecv, left).wait_send()
+
+        return 0
+
+    lax.fori_loop(0, steps, drain, 0)
+
+
+def chain(gam, local, back):
+    heads = gam.shape[0]
+    steps = min(8, heads)
+    spec = pl.BlockSpec(memory_space=pltpu.VMEM)
+    out = jax.ShapeDtypeStruct(local.shape, F32)
+    return pl.pallas_call(
+        chain_kernel,
+        in_specs=[spec] * 3,
+        out_specs=[spec] * 2,
+        out_shape=[out, out],
+        scratch_shapes=[pltpu.VMEM(local.shape, F32)] * 4 + [pltpu.SemaphoreType.DMA((steps,))] * 4,
+        compiler_params=pltpu.CompilerParams(
+            collective_id=0, has_side_effects=True, vmem_limit_bytes=VMEM_LIMIT
+        ),
+    )(gam, local, back)
+
+
+def pair_kernel(gb_ref, gc_ref, ob_ref, oc_ref, got_b, got_c, send, recv):
+    other = {"head": 1 - lax.axis_index("head")}
+    barrier = pltpu.get_barrier_semaphore()
+    pl.semaphore_signal(barrier, inc=1, device_id=other, device_id_type=MESH)
+    pl.semaphore_wait(barrier, 1)
+    pieces = send.shape[1]
+    rows = gb_ref.shape[0] // pieces
+    trio = ((gb_ref, got_b, ob_ref), (gc_ref, got_c, oc_ref))
+
+    def hop(i, k):
+        sl = slice(k * rows, (k + 1) * rows)
+        return pltpu.make_async_remote_copy(
+            src_ref=trio[i][0].at[sl], dst_ref=trio[i][1].at[sl], send_sem=send.at[i, k],
+            recv_sem=recv.at[i, k], device_id=other, device_id_type=MESH,
+        )
+
+    copies = [(i, k, hop(i, k)) for i in range(2) for k in range(pieces)]
+    for _, _, copy in copies:
+        copy.start()
+    for i, k, copy in copies:
+        sl = slice(k * rows, (k + 1) * rows)
+        copy.wait_recv()
+        trio[i][2][sl] = trio[i][0][sl] + trio[i][1][sl]
+    for _, _, copy in copies:
+        copy.wait_send()
+
+
+def over_heads(grad_b, grad_c):
+    if lax.axis_size("head") != 2:
+        return lax.psum((grad_b, grad_c), "head")
+    spec = pl.BlockSpec(memory_space=pltpu.VMEM)
+    out = jax.ShapeDtypeStruct(grad_b.shape, F32)
+    return pl.pallas_call(
+        pair_kernel,
+        in_specs=[spec] * 2,
+        out_specs=[spec] * 2,
+        out_shape=[out, out],
+        scratch_shapes=[pltpu.VMEM(grad_b.shape, F32)] * 2 + [pltpu.SemaphoreType.DMA((2, 4))] * 2,
+        compiler_params=pltpu.CompilerParams(
+            collective_id=1, has_side_effects=True, vmem_limit_bytes=VMEM_LIMIT
+        ),
+    )(grad_b, grad_c)
 
 
 def on_device(
@@ -224,8 +368,7 @@
     )(
         activations, cotangent, b_proj, c_proj, dt_raw, resets[None], agents[None], agent_bias, alog
     )
-    entry = entering((gam, local), ("seq", "rep"), False)
-    exit_grad = entering((gam, back), ("seq", "rep"), True)
+    entry, exit_grad = chain(gam, local, back)
     grad_x, grad_b, grad_c, grad_rate = pl.pallas_call(
         partial(grad_kernel, nb),
         grid=(heads,),
@@ -251,7 +394,7 @@
         activations, cotangent, b_proj, c_proj, rows, aux, added, inject, entry, exit_grad, alog,
         d_skip,
     )
-    grad_b, grad_c = lax.psum((grad_b, grad_c), "head")
+    grad_b, grad_c = over_heads(grad_b, grad_c)
     return (grad_x, grad_b, grad_c, grad_rate)
 
 

time: 282 us -> 112 us (0.40)
  waiting for transfers between devices: 186 us -> 0 us
  Pallas kernels: 46 us -> 102 us
  blocking collectives: 17.2 us -> 0 us
  between operations: 13.8 us -> 0.67 us
  other arithmetic: 9.35 us -> 0 us
    all_gather x2 -> x0, waiting for transfers between devices: 146 us -> none  [entering(): decay, state = jax.tree.map(lambda part: lax.all_gather(part, axis), value)]
    pallas_call x0 -> x2, Pallas kernels: none -> 56.3 us  [the longest x1 31 us: chain(): pl.pallas_call(chain_kernel, in_specs=[spec] * 3, out_specs=[spec] * 2, o...]
    psum x1 -> x0, waiting for transfers between devices: 38.9 us -> none  [on_device(): grad_b, grad_c = lax.psum((grad_b, grad_c), 'head')]
    all_gather x1 -> x0, blocking collectives: 17.2 us -> none  [entering(): decay, state = jax.tree.map(lambda part: lax.all_gather(part, axis), value)]
    select_n x2 -> x0, other arithmetic: 9.31 us -> none  [entering(): total = jnp.where(k < mine, longer, total)]
    unnamed x20 -> x24, local copies, waits for them, and re-layouts: 8.55 us -> 8.37 us
  transfers between devices with their start and end apart: 3 -> 0, of which waited for: 3 -> 0; matrix products, arithmetic and copies ran while one was open for 1% -> 0% of each run, Pallas kernels for 0% -> 0%
where the time goes in v2:
time: 112 us
  Pallas kernels  102 us (91%)
  local copies, waits for them, and re-layouts  9.11 us (8%)
    pallas_call x1, Pallas kernels, chain(): pl.pallas_call(chain_kernel, in_specs=[spec] * 3, out_specs=[spec] * 2, o...  31 us
    pallas_call x1, Pallas kernels, on_device(): pl.pallas_call(partial(grad_kernel, nb), grid=(heads,), in_specs=[xspec,...  30.4 us
    pallas_call x1, Pallas kernels, over_heads(): pl.pallas_call(pair_kernel, in_specs=[spec] * 2, out_specs=[spec] * 2, ou...  25.3 us
    pallas_call x1, Pallas kernels, on_device(): pl.pallas_call(partial(summary_kernel, nb), grid=(heads,), in_specs=[xspe...  15.1 us
    unnamed x24, local copies, waits for them, and re-layouts  8.37 us

profile of v2, /device:TPU:0, one launch (start us, length us, event | category | flops | bytes accessed | tf_op | source)
XLA Modules:
  0.0 111.6 jit_solution(10412026870913263004)
XLA Ops:
  0.6 0.7 copy.14.alog_ref
  1.4 0.0 copy-start
  1.4 0.9 copy-done
  2.3 0.0 copy-start.2
  2.3 0.9 copy-done.2
  3.3 0.0 copy-start.6
  3.3 0.8 copy-done.6
  4.1 0.0 copy-start.7
  4.1 0.7 copy-done.7
  4.8 0.0 copy-start.8
  4.8 0.7 copy-done.8
  5.5 0.0 copy-start.9
  5.5 0.7 copy-done.9
  6.2 0.0 copy-start.1
  6.2 0.0 copy-start.3
  6.2 0.0 copy-start.10
  6.2 15.1 %shard_map.129 = (f32[16,16,256]{2,1,0:T(8,128)S(1)}, f32[3,16,1024]{2,1,0:T(8,128)S(1)}, f32[16,4,128,128]{3,2,1,0:T(8,128)}, bf16[16,4,128,128]{3,2,1,0:T(8,12...) custom-call(bf16[1024,2048]{1,0:T(8,128)(2,1)} %x_ref.3, ...), custom_call_target="tpu_custom_call" | custom-call | tf_op jit(solution)/shard_map/pallas_call | solution.py:350
  21.3 0.0 copy-start.5
  21.3 1.0 copy-done.5
  22.2 31.0 %shard_map.130 = (f32[16,128,128]{2,1,0:T(8,128)S(1)}, f32[16,128,128]{2,1,0:T(8,128)S(1)}) custom-call(f32[16,8,128]{2,1,0:T(8,128)S(1)} %get-tuple-element.23.gam_ref, f32[16,128,128]{2,1,0:T(8,128)S(1)} %get-tuple-element.24.local_ref, f32[16,128,128]{2,1,0:T(8,128)} %copy-done.5), custom_call_target="tpu_custom_call" | custom-call | tf_op jit(solution)/shard_map/pallas_call | solution.py:283
  53.3 0.0 copy-start.4
  53.3 1.0 copy-done.4
  54.3 0.0 copy-done.1
  54.3 0.0 copy-done.3
  54.3 0.0 copy-done.10
  54.3 30.4 %shard_map.131 = (bf16[1024,2048]{1,0:T(8,128)(2,1)}, f32[1024,128]{1,0:T(8,128)S(1)}, f32[1024,128]{1,0:T(8,128)S(1)}, f32[16,1024]{1,0:T(8,128)}) custom-call(bf16[1024,2048]{1,0:T(8,128)(2,1)} %x_ref.3, bf16[1024,2048]{1,0:T(8,128)(2,1)} %dy_ref.3, bf16[1024,128]{1,0:T(8,128)(2,1)S(1)} %copy-done.1, bf16[1024,128]{1,0:T(8,128)(2,1)S(1)} %copy-done.3, ...), custom_call_target="tpu_custom_call" | custom-call | tf_op jit(solution)/shard_map/pallas_call | solution.py:372
  84.7 25.3 %shard_map.132 = (f32[1024,128]{1,0:T(8,128)S(1)}, f32[1024,128]{1,0:T(8,128)S(1)}) custom-call(f32[1024,128]{1,0:T(8,128)S(1)} %get-tuple-element.29.gb_ref, f32[1024,128]{1,0:T(8,128)S(1)} %get-tuple-element.30.gc_ref), custom_call_target="tpu_custom_call" | custom-call | tf_op jit(solution)/shard_map/pallas_call | solution.py:327
  110.0 0.8 copy.18
  110.8 0.8 copy.19
Async XLA Ops:
  1.4 0.9 copy-start
  2.3 0.9 copy-start.2
  3.3 0.8 copy-start.6
  4.1 0.7 copy-start.7
  4.8 0.7 copy-start.8
  5.5 0.7 copy-start.9
  6.2 48.1 %copy-start.1 = (bf16[1024,128]{1,0:T(8,128)(2,1)S(1)}, bf16[1024,128]{1,0:T(8,128)(2,1)}, u32[]{:S(2)}) copy-start(bf16[1024,128]{1,0:T(8,128)(2,1)} %b_ref.3) | copy-start | bytes 786436
  6.2 48.1 %copy-start.3 = (bf16[1024,128]{1,0:T(8,128)(2,1)S(1)}, bf16[1024,128]{1,0:T(8,128)(2,1)}, u32[]{:S(2)}) copy-start(bf16[1024,128]{1,0:T(8,128)(2,1)} %c_ref.3) | copy-start | bytes 786436
  6.2 48.1 %copy-start.10 = (f32[16]{0:T(128)S(1)}, f32[16]{0:T(128)}, u32[]{:S(2)}) copy-start(f32[16]{0:T(128)} %dskip_ref.1) | copy-start | bytes 196
  21.3 1.0 copy-start.5
  53.3 1.0 copy-start.4

commit v3 on v2

--- a/solution.py
+++ b/solution.py
@@ -13,7 +13,7 @@
 F32 = jnp.float32
 BF16 = jnp.bfloat16
 NT = (((1,), (1,)), ((), ()))
-VMEM_LIMIT = 50 * 1024 * 1024
+VMEM_LIMIT = 62 * 1024 * 1024
 
 
 def dot(a, b):
@@ -91,9 +91,9 @@
 
 def grad_kernel(
     nb, x_ref, dy_ref, b_ref, c_ref, rows_ref, aux_ref, added_ref, inject_ref,
-    entry_ref, exit_ref, alog_ref, dskip_ref,
+    entry_ref, exit_ref, alog_ref, dskip_ref, dxi_ref, ds_ref, row_ref,
     gx_ref, gb_ref, gc_ref, gr_ref,
-    bt_s, ct_s, st_s, ds_s, dbt_s, dct_s, drow_s, dcol_s,
+    bt_s, ct_s, dbt_s, dct_s, drow_s, dcol_s,
 ):
     h = pl.program_id(0)
 
@@ -103,13 +103,6 @@
             sl = slice(b * BLOCK, (b + 1) * BLOCK)
             bt_s[:, sl] = b_ref[sl, :].astype(F32).T
             ct_s[:, sl] = c_ref[sl, :].astype(F32).T
-            ep = aux_ref[2, :8, sl]
-            ep_col = ep.T[:, :1]
-            mask = (iota((BLOCK, BLOCK), 0) <= iota((BLOCK, BLOCK), 1)) & (
-                jnp.abs(ep_col - ep[:1]) < 0.5
-            )
-            st_s[b] = jnp.where(mask, dot_nt(b_ref[sl, :], c_ref[sl, :]), 0.0)
-        ds_s[...] = jnp.zeros_like(ds_s)
         dbt_s[...] = jnp.zeros_like(dbt_s)
         dct_s[...] = jnp.zeros_like(dct_s)
 
@@ -129,17 +122,12 @@
         x, dy = x_ref[sl, :], dy_ref[sl, :]
         g16 = grads[b].astype(BF16)
         s16 = states[b].astype(BF16)
-        dmt = dot_nt(x, dy)
-        decay = jnp.exp2(rows[b : b + 1] - cols[:, nb + b : nb + b + 1])
-        mt = st_s[b] * decay
-        ds_s[b] += dmt * decay
-        row = jnp.sum(dmt * mt, axis=0, keepdims=True)
         dcs = dot_nt(s16, dy) * rows[2 * nb + b : 2 * nb + b + 1]
         dct_s[:, sl] += dcs
-        row += jnp.sum(dcs * ct_s[:, sl], axis=0, keepdims=True)
+        row = row_ref[pl.ds(h, 1), sl] + jnp.sum(dcs * ct_s[:, sl], axis=0, keepdims=True)
         row_end = jnp.sum(jnp.sum(grads[b] * states[b + 1], axis=0, keepdims=True), axis=1, keepdims=True)
         dbt_s[:, sl] += dot_nt(g16, x) * rows[3 * nb + b : 3 * nb + b + 1]
-        dx = dot(mt.astype(BF16), dy) + cols[:, 3 * nb + b : 3 * nb + b + 1] * dot(b_ref[sl, :], g16)
+        dx = dxi_ref[sl, :].astype(F32) + cols[:, 3 * nb + b : 3 * nb + b + 1] * dot(b_ref[sl, :], g16)
         z = x.astype(F32) * dx
         zh = z.astype(BF16)
         zl = (z - zh.astype(F32)).astype(BF16)
@@ -162,7 +150,7 @@
             mask = (iota((BLOCK, BLOCK), 0) <= iota((BLOCK, BLOCK), 1)) & (
                 jnp.abs(ep_col - ep[:1]) < 0.5
             )
-            ds = jnp.where(mask, ds_s[b], 0.0)
+            ds = jnp.where(mask, ds_ref[b], 0.0)
             dh = ds.astype(BF16)
             dl = (ds - dh.astype(F32)).astype(BF16)
             ct = ct_s[:, sl].astype(BF16)
@@ -184,14 +172,17 @@
 
 
 def chain_kernel(
-    gam_ref, local_ref, back_ref, entry_ref, exit_ref,
+    gam_ref, local_ref, back_ref, x_ref, dy_ref, b_ref, c_ref, rows_ref, aux_ref,
+    entry_ref, exit_ref, dxi_ref, ds_ref, row_ref, st_s,
     fin_s, fout_s, bin_s, bout_s, fsend, frecv, bsend, brecv,
 ):
     reps = lax.axis_size("rep")
     last = lax.axis_size("seq") * reps - 1
     mine = lax.axis_index("seq") * reps + lax.axis_index("rep")
     steps = fsend.shape[0]
-    per = gam_ref.shape[0] // steps
+    heads, _, width = gam_ref.shape
+    per = heads // steps
+    nb = ds_ref.shape[0]
 
     def place(index):
         return {"seq": index // reps, "rep": index % reps}
@@ -245,6 +236,29 @@
     right = jnp.minimum(mine + 1, last)
     left = jnp.maximum(mine - 1, 0)
 
+    for b in range(nb):
+        sl = slice(b * BLOCK, (b + 1) * BLOCK)
+        ep = aux_ref[2, :8, sl]
+        mask = (iota((BLOCK, BLOCK), 0) <= iota((BLOCK, BLOCK), 1)) & (
+            jnp.abs(ep.T[:, :1] - ep[:1]) < 0.5
+        )
+        st_s[b] = jnp.where(mask, dot_nt(b_ref[sl, :], c_ref[sl, :]), 0.0)
+    ds_ref[...] = jnp.zeros_like(ds_ref)
+
+    def within_blocks(h):
+        rows = rows_ref[h]
+        cols = rows[: 2 * nb].T
+        lanes = pl.ds(pl.multiple_of(h * width, width), width)
+        for b in range(nb):
+            sl = slice(b * BLOCK, (b + 1) * BLOCK)
+            dy = dy_ref[sl, lanes]
+            dmt = dot_nt(x_ref[sl, lanes], dy)
+            decay = jnp.exp2(rows[b : b + 1] - cols[:, nb + b : nb + b + 1])
+            mt = st_s[b] * decay
+            ds_ref[b] += dmt * decay
+            row_ref[pl.ds(h, 1), sl] = jnp.sum(dmt * mt, axis=0, keepdims=True)
+            dxi_ref[sl, lanes] = dot(mt.astype(BF16), dy).astype(BF16)
+
     def tick(t, _):
         kf = t - mine * AHEAD
         kb = t - (last - mine) * AHEAD
@@ -257,9 +271,13 @@
         def _():
             advance(kb, mine == last, mine == 0, left, back_ref, exit_ref, bout_s, bin_s, bsend, brecv)
 
+        @pl.when(t < heads)
+        def _():
+            within_blocks(t)
+
         return 0
 
-    lax.fori_loop(0, last * AHEAD + steps, tick, 0)
+    lax.fori_loop(0, max(last * AHEAD + steps, heads), tick, 0)
 
     def drain(k, _):
         @pl.when(mine < last)
@@ -275,21 +293,26 @@
     lax.fori_loop(0, steps, drain, 0)
 
 
-def chain(gam, local, back):
+def chain(gam, local, back, x, dy, b_proj, c_proj, rows, aux):
     heads = gam.shape[0]
+    tokens = x.shape[0]
+    pieces = jax.ShapeDtypeStruct((tokens // BLOCK, BLOCK, BLOCK), F32)
     steps = min(8, heads)
     spec = pl.BlockSpec(memory_space=pltpu.VMEM)
     out = jax.ShapeDtypeStruct(local.shape, F32)
     return pl.pallas_call(
         chain_kernel,
-        in_specs=[spec] * 3,
-        out_specs=[spec] * 2,
-        out_shape=[out, out],
-        scratch_shapes=[pltpu.VMEM(local.shape, F32)] * 4 + [pltpu.SemaphoreType.DMA((steps,))] * 4,
+        in_specs=[spec] * 9,
+        out_specs=[spec] * 5,
+        out_shape=[
+            out, out, jax.ShapeDtypeStruct(x.shape, BF16), pieces,
+            jax.ShapeDtypeStruct((heads, tokens), F32),
+        ],
+        scratch_shapes=[pltpu.VMEM(pieces.shape, F32)] + [pltpu.VMEM(local.shape, F32)] * 4 + [pltpu.SemaphoreType.DMA((steps,))] * 4,
         compiler_params=pltpu.CompilerParams(
             collective_id=0, has_side_effects=True, vmem_limit_bytes=VMEM_LIMIT
         ),
-    )(gam, local, back)
+    )(gam, local, back, x, dy, b_proj, c_proj, rows, aux)
 
 
 def pair_kernel(gb_ref, gc_ref, ob_ref, oc_ref, got_b, got_c, send, recv):
@@ -368,7 +391,9 @@
     )(
         activations, cotangent, b_proj, c_proj, dt_raw, resets[None], agents[None], agent_bias, alog
     )
-    entry, exit_grad = chain(gam, local, back)
+    entry, exit_grad, dxi, ds, drow = chain(
+        gam, local, back, activations, cotangent, b_proj, c_proj, rows, aux
+    )
     grad_x, grad_b, grad_c, grad_rate = pl.pallas_call(
         partial(grad_kernel, nb),
         grid=(heads,),
@@ -376,7 +401,8 @@
             xspec, xspec, whole((tokens, n)), whole((tokens, n)), per_head((4 * nb, BLOCK)),
             whole((3, heads, tokens)), per_head((nb, n, width)), per_head((nb, n, width)),
             per_head((n, width)), per_head((n, width)), whole((heads, 1)),
-            pl.BlockSpec(memory_space=pltpu.SMEM),
+            pl.BlockSpec(memory_space=pltpu.SMEM), xspec, whole((nb, BLOCK, BLOCK)),
+            whole((heads, tokens)),
         ],
         out_specs=[xspec, whole((tokens, n)), whole((tokens, n)), whole((heads, tokens))],
         out_shape=[
@@ -385,14 +411,13 @@
         ],
         scratch_shapes=[
             pltpu.VMEM((n, tokens), F32), pltpu.VMEM((n, tokens), F32),
-            pltpu.VMEM((nb, BLOCK, BLOCK), F32), pltpu.VMEM((nb, BLOCK, BLOCK), F32),
             pltpu.VMEM((n, tokens), F32), pltpu.VMEM((n, tokens), F32),
             pltpu.VMEM((heads, tokens), F32), pltpu.VMEM((heads, tokens), F32),
         ],
         compiler_params=pltpu.CompilerParams(vmem_limit_bytes=VMEM_LIMIT),
     )(
         activations, cotangent, b_proj, c_proj, rows, aux, added, inject, entry, exit_grad, alog,
-        d_skip,
+        d_skip, dxi, ds, drow,
     )
     grad_b, grad_c = over_heads(grad_b, grad_c)
     return (grad_x, grad_b, grad_c, grad_rate)

time: 112 us -> 114 us (1.018)
  Pallas kernels: 102 us -> 108 us
  local copies, waits for them, and re-layouts: 9.11 us -> 5.06 us
    pallas_call x1, Pallas kernels: 31 us -> 38.9 us  [chain(): pl.pallas_call(chain_kernel, in_specs=[spec] * 9, out_specs=[spec] * 5, o...]
    pallas_call x1, Pallas kernels: 30.4 us -> 25.4 us  [on_device(): pl.pallas_call(partial(grad_kernel, nb), grid=(heads,), in_specs=[xspec,...]
    unnamed x24 -> x2, local copies, waits for them, and re-layouts: 8.37 us -> 3.74 us
    pallas_call x1, Pallas kernels: 25.3 us -> 27.5 us  [over_heads(): pl.pallas_call(pair_kernel, in_specs=[spec] * 2, out_specs=[spec] * 2, ou...]
where the time goes in v3:
time: 114 us; the launch traced here: 113 us
  Pallas kernels  108 us (95%)
  local copies, waits for them, and re-layouts  5.06 us (4%)
    pallas_call x1, Pallas kernels, chain(): pl.pallas_call(chain_kernel, in_specs=[spec] * 9, out_specs=[spec] * 5, o...  38.9 us
    pallas_call x1, Pallas kernels, over_heads(): pl.pallas_call(pair_kernel, in_specs=[spec] * 2, out_specs=[spec] * 2, ou...  27.5 us
    pallas_call x1, Pallas kernels, on_device(): pl.pallas_call(partial(grad_kernel, nb), grid=(heads,), in_specs=[xspec,...  25.4 us
    pallas_call x1, Pallas kernels, on_device(): pl.pallas_call(partial(summary_kernel, nb), grid=(heads,), in_specs=[xspe...  15.7 us
    unnamed x2, local copies, waits for them, and re-layouts  3.74 us

profile of v3, /device:TPU:0, one launch (start us, length us, event | category | flops | bytes accessed | tf_op | source)
XLA Modules:
  0.0 113.2 jit_solution(7995616381047284968)
XLA Ops:
  0.6 1.3 %copy.14.alog_ref = f32[16,1]{1,0:T(8,128)} copy(f32[16,1]{0,1:T(1,128)} %bitcast.5) | data formatting | bytes 128 | tf_op jit(solution)/shard_map/broadcast_in_dim | solution.py:371
  2.0 15.7 %shard_map.129 = (f32[16,16,256]{2,1,0:T(8,128)}, f32[3,16,1024]{2,1,0:T(8,128)}, f32[16,4,128,128]{3,2,1,0:T(8,128)}, bf16[16,4,128,128]{3,2,1,0:T(8,128)(2,1)}...) custom-call(bf16[1024,2048]{1,0:T(8,128)(2,1)} %x_ref.5, bf16[1024,2048]{1,0:T(8,128)(2,1)} %dy_ref.5, ...), custom_call_target="tpu_custom_call" | custom-call | tf_op jit(solution)/shard_map/pallas_call | solution.py:373
  17.6 38.9 %shard_map.130 = (f32[16,128,128]{2,1,0:T(8,128)}, f32[16,128,128]{2,1,0:T(8,128)}, bf16[1024,2048]{1,0:T(8,128)(2,1)}, f32[4,256,256]{2,1,0:T(8,128)}, f32[16,1024]{1,0:T(8,128)}) custom-call(f32[16,8,128]{2,1,0:T(8,128)} %get-tuple-element.26.gam_ref, f32[16,128,128]{2,1,0:T(8,128)} %get-tuple-element.27.local_ref, ...), custom_call_target="tpu_custom_call" | custom-call | tf_op jit(solution)/shard_map/pallas_call | solution.py:303
  56.6 25.4 %shard_map.131 = (bf16[1024,2048]{1,0:T(8,128)(2,1)}, f32[1024,128]{1,0:T(8,128)}, f32[1024,128]{1,0:T(8,128)}, f32[16,1024]{1,0:T(8,128)}) custom-call(bf16[1024,2048]{1,0:T(8,128)(2,1)} %x_ref.5, bf16[1024,2048]{1,0:T(8,128)(2,1)} %dy_ref.5, bf16[1024,128]{1,0:T(8,128)(2,1)} %b_ref.5, bf16[1024,128]{1,0:T(8,128)(2,1)} %c_ref.5, ...), custom_call_target="tpu_custom_call" | custom-call | tf_op jit(solution)/shard_map/pallas_call | solution.py:397
  82.0 27.5 %shard_map.132 = (f32[1024,128]{1,0:T(8,128)}, f32[1024,128]{1,0:T(8,128)}) custom-call(f32[1024,128]{1,0:T(8,128)} %get-tuple-element.35.gb_ref, f32[1024,128]{1,0:T(8,128)} %get-tuple-element.36.gc_ref), custom_call_target="tpu_custom_call" | custom-call | tf_op jit(solution)/shard_map/pallas_call | solution.py:350
  109.5 1.9 %copy.18 = f32[1024,128]{1,0:T(8,128)} copy(f32[1024,128]{1,0:T(8,128)} %get-tuple-element.45) | data formatting | bytes 1048576
  111.3 1.9 %copy.19 = f32[1024,128]{1,0:T(8,128)} copy(f32[1024,128]{1,0:T(8,128)} %get-tuple-element.46) | data formatting | bytes 1048576

commit v4 on v2

--- a/solution.py
+++ b/solution.py
@@ -13,7 +13,7 @@
 F32 = jnp.float32
 BF16 = jnp.bfloat16
 NT = (((1,), (1,)), ((), ()))
-VMEM_LIMIT = 50 * 1024 * 1024
+VMEM_LIMIT = 62 * 1024 * 1024
 
 
 def dot(a, b):
@@ -180,7 +180,7 @@
 
 
 MESH = pl.DeviceIdType.MESH
-AHEAD = 2
+AHEAD = 4
 
 
 def chain_kernel(
@@ -277,7 +277,7 @@
 
 def chain(gam, local, back):
     heads = gam.shape[0]
-    steps = min(8, heads)
+    steps = heads
     spec = pl.BlockSpec(memory_space=pltpu.VMEM)
     out = jax.ShapeDtypeStruct(local.shape, F32)
     return pl.pallas_call(

time: 112 us -> 113 us (level)
  local copies, waits for them, and re-layouts: 9.11 us -> 5.06 us
  Pallas kernels: 102 us -> 106 us
    unnamed x24 -> x2, local copies, waits for them, and re-layouts: 8.37 us -> 3.74 us
    pallas_call x1, Pallas kernels: 25.3 us -> 27.4 us  [over_heads(): pl.pallas_call(pair_kernel, in_specs=[spec] * 2, out_specs=[spec] * 2, ou...]
    pallas_call x1, Pallas kernels: 31 us -> 32.2 us  [chain(): pl.pallas_call(chain_kernel, in_specs=[spec] * 3, out_specs=[spec] * 2, o...]
where the time goes in v4:
time: 113 us; the launch traced here: 112 us
  Pallas kernels  106 us (94%)
  local copies, waits for them, and re-layouts  5.06 us (4%)
    pallas_call x1, Pallas kernels, chain(): pl.pallas_call(chain_kernel, in_specs=[spec] * 3, out_specs=[spec] * 2, o...  32.2 us
    pallas_call x1, Pallas kernels, on_device(): pl.pallas_call(partial(grad_kernel, nb), grid=(heads,), in_specs=[xspec,...  31 us
    pallas_call x1, Pallas kernels, over_heads(): pl.pallas_call(pair_kernel, in_specs=[spec] * 2, out_specs=[spec] * 2, ou...  27.4 us
    pallas_call x1, Pallas kernels, on_device(): pl.pallas_call(partial(summary_kernel, nb), grid=(heads,), in_specs=[xspe...  15.7 us
    unnamed x2, local copies, waits for them, and re-layouts  3.74 us

profile of v4, /device:TPU:0, one launch (start us, length us, event | category | flops | bytes accessed | tf_op | source)
XLA Modules:
  0.0 112.1 jit_solution(17928877926846654040)
XLA Ops:
  0.6 1.3 %copy.14.alog_ref = f32[16,1]{1,0:T(8,128)} copy(f32[16,1]{0,1:T(1,128)} %bitcast.5) | data formatting | bytes 128 | tf_op jit(solution)/shard_map/broadcast_in_dim | solution.py:348
  2.0 15.7 %shard_map.129 = (f32[16,16,256]{2,1,0:T(8,128)}, f32[3,16,1024]{2,1,0:T(8,128)}, f32[16,4,128,128]{3,2,1,0:T(8,128)}, bf16[16,4,128,128]{3,2,1,0:T(8,128)(2,1)}...) custom-call(bf16[1024,2048]{1,0:T(8,128)(2,1)} %x_ref.3, bf16[1024,2048]{1,0:T(8,128)(2,1)} %dy_ref.3, ...), custom_call_target="tpu_custom_call" | custom-call | tf_op jit(solution)/shard_map/pallas_call | solution.py:350
  17.6 32.2 %shard_map.130 = (f32[16,128,128]{2,1,0:T(8,128)}, f32[16,128,128]{2,1,0:T(8,128)}) custom-call(f32[16,8,128]{2,1,0:T(8,128)} %get-tuple-element.23.gam_ref, f32[16,128,128]{2,1,0:T(8,128)} %get-tuple-element.24.local_ref, f32[16,128,128]{2,1,0:T(8,128)} %get-tuple-element.25.back_ref), custom_call_target="tpu_custom_call" | custom-call | tf_op jit(solution)/shard_map/pallas_call | solution.py:283
  49.9 31.0 %shard_map.131 = (bf16[1024,2048]{1,0:T(8,128)(2,1)}, f32[1024,128]{1,0:T(8,128)}, f32[1024,128]{1,0:T(8,128)}, f32[16,1024]{1,0:T(8,128)}) custom-call(bf16[1024,2048]{1,0:T(8,128)(2,1)} %x_ref.3, bf16[1024,2048]{1,0:T(8,128)(2,1)} %dy_ref.3, bf16[1024,128]{1,0:T(8,128)(2,1)} %b_ref.3, bf16[1024,128]{1,0:T(8,128)(2,1)} %c_ref.3, ...), custom_call_target="tpu_custom_call" | custom-call | tf_op jit(solution)/shard_map/pallas_call | solution.py:372
  80.9 27.4 %shard_map.132 = (f32[1024,128]{1,0:T(8,128)}, f32[1024,128]{1,0:T(8,128)}) custom-call(f32[1024,128]{1,0:T(8,128)} %get-tuple-element.29.gb_ref, f32[1024,128]{1,0:T(8,128)} %get-tuple-element.30.gc_ref), custom_call_target="tpu_custom_call" | custom-call | tf_op jit(solution)/shard_map/pallas_call | solution.py:327
  108.4 1.9 %copy.18 = f32[1024,128]{1,0:T(8,128)} copy(f32[1024,128]{1,0:T(8,128)} %get-tuple-element.39) | data formatting | bytes 1048576
  110.2 1.9 %copy.19 = f32[1024,128]{1,0:T(8,128)} copy(f32[1024,128]{1,0:T(8,128)} %get-tuple-element.40) | data formatting | bytes 1048576

commit v5 on v2

--- a/solution.py
+++ b/solution.py
@@ -141,9 +141,7 @@
         dbt_s[:, sl] += dot_nt(g16, x) * rows[3 * nb + b : 3 * nb + b + 1]
         dx = dot(mt.astype(BF16), dy) + cols[:, 3 * nb + b : 3 * nb + b + 1] * dot(b_ref[sl, :], g16)
         z = x.astype(F32) * dx
-        zh = z.astype(BF16)
-        zl = (z - zh.astype(F32)).astype(BF16)
-        col = (dot_nt(ones, zh) + dot_nt(ones, zl))[:1]
+        col = dot_nt(ones, z.astype(BF16))[:1]
         gx_ref[sl, :] = (dx + d_h * dy.astype(F32)).astype(BF16)
         last = iota((1, BLOCK), 1) == BLOCK - 1
         drow_s[pl.ds(h, 1), sl] = row - col + jnp.where(last, row_end, 0.0)
@@ -364,7 +362,7 @@
             sds((heads, n, width), F32), sds((heads, n, width), F32), sds((heads, 8, width), F32),
         ],
         scratch_shapes=[pltpu.VMEM((n, tokens), F32), pltpu.VMEM((n, tokens), F32)],
-        compiler_params=pltpu.CompilerParams(vmem_limit_bytes=VMEM_LIMIT),
+        compiler_params=pltpu.CompilerParams(vmem_limit_bytes=62 * 1024 * 1024),
     )(
         activations, cotangent, b_proj, c_proj, dt_raw, resets[None], agents[None], agent_bias, alog
     )

time: 112 us -> 109 us (0.973)
  Pallas kernels: 102 us -> 99.7 us
  local copies, waits for them, and re-layouts: 9.11 us -> 7.83 us
    pallas_call x1, Pallas kernels: 30.4 us -> 27.7 us  [on_device(): pl.pallas_call(partial(grad_kernel, nb), grid=(heads,), in_specs=[xspec,...]
    unnamed x24 -> x20, local copies, waits for them, and re-layouts: 8.37 us -> 6.51 us
where the time goes in v5:
time: 109 us; the launch traced here: 108 us
  Pallas kernels  99.7 us (91%)
  local copies, waits for them, and re-layouts  7.83 us (7%)
    pallas_call x1, Pallas kernels, chain(): pl.pallas_call(chain_kernel, in_specs=[spec] * 3, out_specs=[spec] * 2, o...  31 us
    pallas_call x1, Pallas kernels, on_device(): pl.pallas_call(partial(grad_kernel, nb), grid=(heads,), in_specs=[xspec,...  27.7 us
    pallas_call x1, Pallas kernels, over_heads(): pl.pallas_call(pair_kernel, in_specs=[spec] * 2, out_specs=[spec] * 2, ou...  25.3 us
    pallas_call x1, Pallas kernels, on_device(): pl.pallas_call(partial(summary_kernel, nb), grid=(heads,), in_specs=[xspe...  15.8 us
    unnamed x20, local copies, waits for them, and re-layouts  6.51 us

profile of v5, /device:TPU:0, one launch (start us, length us, event | category | flops | bytes accessed | tf_op | source)
XLA Modules:
  0.0 108.3 jit_solution(3129343359579200055)
XLA Ops:
  0.6 1.3 %copy.14.alog_ref = f32[16,1]{1,0:T(8,128)} copy(f32[16,1]{0,1:T(1,128)} %bitcast.5) | data formatting | bytes 128 | tf_op jit(solution)/shard_map/broadcast_in_dim | solution.py:346
  2.0 0.0 copy-start
  2.0 0.0 copy-start.1
  2.0 0.0 copy-start.6
  2.0 0.0 copy-start.8
  2.0 15.8 %shard_map.129 = (f32[16,16,256]{2,1,0:T(8,128)}, f32[3,16,1024]{2,1,0:T(8,128)}, f32[16,4,128,128]{3,2,1,0:T(8,128)}, bf16[16,4,128,128]{3,2,1,0:T(8,128)(2,1)}...) custom-call(bf16[1024,2048]{1,0:T(8,128)(2,1)} %x_ref.3, bf16[1024,2048]{1,0:T(8,128)(2,1)} %dy_ref.3, ...), custom_call_target="tpu_custom_call" | custom-call | tf_op jit(solution)/shard_map/pallas_call | solution.py:348
  17.7 0.0 copy-start.3
  17.7 1.2 %copy-done.3 = f32[16,128,128]{2,1,0:T(8,128)S(1)} copy-done((f32[16,128,128]{2,1,0:T(8,128)S(1)}, f32[16,128,128]{2,1,0:T(8,128)}, u32[]{:S(2)}) %copy-start.3) | copy-done | bytes 1048600
  19.0 0.0 copy-start.7
  19.0 0.8 copy-done.7
  19.8 31.0 %shard_map.130 = (f32[16,128,128]{2,1,0:T(8,128)S(1)}, f32[16,128,128]{2,1,0:T(8,128)S(1)}) custom-call(f32[16,8,128]{2,1,0:T(8,128)S(1)} %copy-done.7, f32[16,128,128]{2,1,0:T(8,128)S(1)} %copy-done.3, f32[16,128,128]{2,1,0:T(8,128)} %get-tuple-element.25.back_ref), custom_call_target="tpu_custom_call" | custom-call | tf_op jit(solution)/shard_map/pallas_call | solution.py:281
  50.8 0.0 copy-start.2
  50.8 1.0 copy-done.2
  51.8 0.0 copy-done
  51.8 0.0 copy-done.1
  51.8 0.0 copy-done.6
  51.8 0.0 copy-done.8
  51.8 0.0 copy-start.4
  51.8 0.9 copy-done.4
  52.8 0.0 copy-start.5
  52.8 0.9 copy-done.5
  53.7 27.7 %shard_map.131 = (bf16[1024,2048]{1,0:T(8,128)(2,1)}, f32[1024,128]{1,0:T(8,128)S(1)}, f32[1024,128]{1,0:T(8,128)S(1)}, f32[16,1024]{1,0:T(8,128)}) custom-call(bf16[1024,2048]{1,0:T(8,128)(2,1)} %x_ref.3, bf16[1024,2048]{1,0:T(8,128)(2,1)} %dy_ref.3, bf16[1024,128]{1,0:T(8,128)(2,1)S(1)} %copy-done, bf16[1024,128]{1,0:T(8,128)(2,1)S(1)} %copy-done.1, ...), custom_call_target="tpu_custom_call" | custom-call | tf_op jit(solution)/shard_map/pallas_call | solution.py:370
  81.4 25.3 %shard_map.132 = (f32[1024,128]{1,0:T(8,128)S(1)}, f32[1024,128]{1,0:T(8,128)S(1)}) custom-call(f32[1024,128]{1,0:T(8,128)S(1)} %get-tuple-element.29.gb_ref, f32[1024,128]{1,0:T(8,128)S(1)} %get-tuple-element.30.gc_ref), custom_call_target="tpu_custom_call" | custom-call | tf_op jit(solution)/shard_map/pallas_call | solution.py:325
  106.7 0.8 copy.18
  107.5 0.8 copy.19
Async XLA Ops:
  2.0 49.9 %copy-start = (bf16[1024,128]{1,0:T(8,128)(2,1)S(1)}, bf16[1024,128]{1,0:T(8,128)(2,1)}, u32[]{:S(2)}) copy-start(bf16[1024,128]{1,0:T(8,128)(2,1)} %b_ref.3) | copy-start | bytes 786436
  2.0 49.9 %copy-start.1 = (bf16[1024,128]{1,0:T(8,128)(2,1)S(1)}, bf16[1024,128]{1,0:T(8,128)(2,1)}, u32[]{:S(2)}) copy-start(bf16[1024,128]{1,0:T(8,128)(2,1)} %c_ref.3) | copy-start | bytes 786436
  2.0 49.9 %copy-start.6 = (f32[16,1]{1,0:T(8,128)S(1)}, f32[16,1]{1,0:T(8,128)}, u32[]{:S(2)}) copy-start(f32[16,1]{1,0:T(8,128)} %copy.14.alog_ref) | copy-start | bytes 196
  2.0 49.9 %copy-start.8 = (f32[16]{0:T(128)S(1)}, f32[16]{0:T(128)}, u32[]{:S(2)}) copy-start(f32[16]{0:T(128)} %dskip_ref.1) | copy-start | bytes 196
  17.7 1.2 %copy-start.3 = (f32[16,128,128]{2,1,0:T(8,128)S(1)}, f32[16,128,128]{2,1,0:T(8,128)}, u32[]{:S(2)}) copy-start(f32[16,128,128]{2,1,0:T(8,128)} %get-tuple-element.24.local_ref) | copy-start | bytes 3145732
  19.0 0.8 copy-start.7
  50.8 1.0 copy-start.2
  51.8 1.0 copy-start.4
  52.8 0.9 copy-start.5
